TPU v7x, 256 devices: a whole 4x4x8 slice. The times are simulated.
256 devices in a mesh: row: 32 (over x_lo, z, core), col: 8 (over x_hi, y).
Axes of the slice: x: 4 (x_hi: 2, x_lo: 2; x = x_hi * 2 + x_lo), y: 4, z: 8, core: 2. Of those that a mesh axis runs over, the one named last changes fastest.
Arguments:
- ham: bfloat16 [8192, 8192], P('row'), may hold values from -0.2 to 1.7, as said below
- coeff: bfloat16 [8192, 8192], P('row', 'col'), may hold values from -40 to 40, as said below
- tile_mask: int32 [256, 256], P('row'), may hold values from 0 to 1, as said below
- occupation: int32 [16, 8192], replicated, may hold values from 0 to 1, as said below
- orbital_energy: float32 [16], replicated, may hold values from -0.4 to 0.6
- coulomb: float32 [16, 16], replicated, may hold values from 0.005 to 0.04
Outputs:
- correction: float32 [8192, 8192], P('row', 'col')
- stats: float32 [2], replicated
Inputs may be any that keep to these rules, and one draw needn't show every extreme that they name: ham is symmetric. coeff is symmetric. tile_mask is symmetric with ones on its diagonal. `occupation`: every column holds exactly 6 ones.
All inputs are finite; a program needn't handle non-finite values.
Results may differ from a plain program's by a relative error of at most 0.0003.
Values may be sent and summed in bfloat16 or wider, within the bound.
No kernel may reach another device: no remote copies, remote signals or barrier semaphores. Data moves between devices by JAX's collectives and lax.ppermute only.
A program may use at most 128 MiB of HBM per device.

v0:
```python
import jax
import jax.numpy as jnp
from jax import lax
from jax.sharding import PartitionSpec as P

NS = 8192


def turn_tiles(product):
    tile_rows, tile_cols = product.shape
    row_count = lax.axis_size("row")
    col_count = lax.axis_size("col")
    fold_count = row_count // col_count
    sub_rows = tile_rows // row_count
    sectioned = product.reshape(row_count, sub_rows, tile_cols)
    sectioned = lax.all_to_all(
        lax.all_to_all(sectioned, "row", split_axis=0, concat_axis=0, tiled=True),
        "col",
        split_axis=0,
        concat_axis=0,
        tiled=True,
    )
    sectioned = sectioned.reshape(col_count, fold_count, sub_rows, fold_count, tile_rows)
    sectioned = jnp.transpose(sectioned, (0, 3, 1, 2, 4)).reshape(
        row_count, fold_count * sub_rows, tile_rows
    )
    sectioned = lax.all_to_all(sectioned, "row", split_axis=0, concat_axis=0, tiled=True)
    sectioned = sectioned.reshape(row_count, fold_count, sub_rows, tile_rows)
    turned = jnp.transpose(sectioned, (3, 1, 0, 2)).reshape(tile_rows, tile_cols)
    return turned


def body(ham, coeff, tile_mask, occupation, orbital_energy, coulomb):
    tile_rows, strings = ham.shape
    tile_cols = coeff.shape[1]
    mask_cols = tile_mask.shape[1]
    block_size = strings // mask_cols
    mask_rows = tile_rows // block_size
    weights = tile_mask.astype(jnp.bfloat16)[:, None, :, None]
    masked = (ham.reshape(mask_rows, block_size, mask_cols, block_size) * weights).reshape(
        tile_rows, strings
    )
    occ_float = occupation.astype(jnp.float32)
    occ_alpha = lax.dynamic_slice_in_dim(occ_float, lax.axis_index("row") * tile_rows, tile_rows, 1)
    occ_beta = lax.dynamic_slice_in_dim(occ_float, lax.axis_index("col") * tile_cols, tile_cols, 1)
    energy_alpha = jnp.dot(orbital_energy, occ_alpha, precision=lax.Precision.HIGHEST)
    energy_beta = jnp.dot(orbital_energy, occ_beta, precision=lax.Precision.HIGHEST)
    coupling = jnp.dot(
        jnp.dot(occ_alpha.T, coulomb, precision=lax.Precision.HIGHEST),
        occ_beta,
        precision=lax.Precision.HIGHEST,
    )
    diagonal = energy_alpha[:, None] + energy_beta[None, :] + coupling
    product = jnp.dot(
        masked, lax.all_gather(coeff, "row", axis=0, tiled=True), preferred_element_type=jnp.float32
    )
    coeff_float = coeff.astype(jnp.float32)
    sigma = product + turn_tiles(product)
    late = lax.psum(
        (jnp.sum(coeff_float * sigma), jnp.sum(coeff_float * coeff_float)), ("row", "col")
    )
    projection = late[0]
    weight_sum = late[1]
    theta = projection / weight_sum
    residual = sigma - theta * coeff_float
    update = residual / jnp.maximum(jnp.abs(diagonal - theta), 1.0)
    totals = lax.psum((jnp.sum(residual * residual), jnp.sum(update * update)), ("row", "col"))
    correction = update * lax.rsqrt(totals[1] / (NS * NS) + 1e-06)
    stats = jnp.stack([theta, jnp.sqrt(totals[0] / (NS * NS))])
    return (correction, stats)


def solution(mesh):
    in_specs = (P("row", None), P("row", "col"), P("row", None), P(), P(), P())
    out_specs = (P("row", "col"), P())
    return jax.shard_map(body, mesh=mesh, in_specs=in_specs, out_specs=out_specs, check_vma=False)
```

profile of v0, /device:TPU:1, one launch (start us, length us, event | category | flops | bytes accessed | tf_op | source)
XLA Modules:
  0.0 381.5 jit_solution(8685659466072624419)
XLA Ops:
  7.2 0.0 copy-start
  7.2 0.0 all-gather.2.cloned.1.call-start
  7.2 0.7 all-gather.2.cloned.1.call-update
  7.9 0.7 convert_element_type.9
  8.6 6.4 %mul.41 = bf16[8,32,256,32]{3,2,1,0:T(8,128)(2,1)} broadcast(bf16[8,256]{1,0:T(8,128)(2,1)S(1)} %convert_element_type.9), dimensions={0,2} | broadcast | bytes 4198400 | tf_op jit(solution)/shard_map/mul | solution.py:40
  15.0 21.9 %mul.42 = bf16[256,8192]{1,0:T(8,128)(2,1)} reshape(bf16[8,32,256,32]{3,2,1,0:T(8,128)(2,1)} %mul.41) | data formatting | bytes 8388608 | tf_op jit(solution)/shard_map/mul | solution.py:40
  36.9 77.0 %all-gather.2.cloned.1.call-done = bf16[8192,1024]{1,0:T(8,128)(2,1)} async-done(((bf16[256,1024]{1,0:T(8,128)(2,1)}), bf16[8192,1024]{1,0:T(8,128)(2,1)}) %all-gather.2.cloned.1.call-update) | async-done | bytes 16777232 | tf_op jit(solution)/shard_map/all_gather | solution.py:55
  113.9 10.5 %fusion = f32[256,1024]{1,0:T(8,128)S(1)} fusion(bf16[8192,1024]{1,0:T(8,128)(2,1)} %all-gather.2.cloned.1.call-done, bf16[256,8192]{1,0:T(8,128)(2,1)} %param.6, bf16[256,8192]{1,0:T(8,128)(2,1)} %mul.42), kind=kOutput, calls=%fused_computation | convolution fusion | flops 4297064448 | bytes 26214400 | tf_op jit(solution)/shard_map/dot_general | solution.py:54
  124.4 0.0 copy-start.2
  124.4 33.6 %all_to_all.15 = f32[32,8,1024]{2,1,0:T(8,128)S(1)} all-to-all(f32[32,8,1024]{2,1,0:T(8,128)S(1)} %bitcast.25), channel_id=1, replica_groups=mesh['row'=32,'col'=8] {'row'}, dimensions={0} | all-to-all | bytes 2097152 | tf_op jit(solution)/shard_map/all_to_all | solution.py:17
  158.0 0.0 copy-done.2
  158.0 0.0 copy-start.3
  158.0 20.1 %all_to_all.16 = f32[32,8,1024]{2,1,0:T(8,128)S(1)} all-to-all(f32[32,8,1024]{2,1,0:T(8,128)S(1)} %all_to_all.15), channel_id=1, replica_groups=mesh['row'=32,'col'=8] {'col'}, dimensions={0} | all-to-all | bytes 2097152 | tf_op jit(solution)/shard_map/all_to_all | solution.py:16
  178.2 0.0 copy-start.4
  178.2 0.5 reshape.26
  178.7 1.2 copy.10
  179.8 0.0 copy-start.1
  179.8 9.1 %all-to-all-start.2 = ((f32[32,32,256]{2,1,0:T(8,128)}), f32[32,32,256]{2,1,0:T(8,128)S(1)}, u32[]{:S(2)}, u32[]{:S(2)}) async-start(f32[32,32,256]{2,1,0:T(8,128)} %bitcast.2), calls=%async_computation.2 | async-start | bytes 2097152 | tf_op jit(solution)/shard_map/all_to_all | solution.py:27
  188.9 0.0 copy-done.3
  189.0 0.0 copy-done.4
  189.0 0.1 fusion.14
  189.1 0.2 fusion.10
  189.3 0.0 copy-done
  189.3 0.2 fusion.12
  189.5 25.9 %all-to-all-done.2 = f32[32,32,256]{2,1,0:T(8,128)S(1)} async-done(((f32[32,32,256]{2,1,0:T(8,128)}), f32[32,32,256]{2,1,0:T(8,128)S(1)}, u32[]{:S(2)}, u32[]{:S(2)}) %all-to-all-start.2) | async-done | bytes 1048608 | tf_op jit(solution)/shard_map/all_to_all | solution.py:27
  215.4 0.1 copy.11
  215.5 1.3 copy.12
  216.8 0.0 copy-done.1
  216.8 2.6 fusion.7
  219.4 74.3 %all-reduce.1 = (f32[]{:T(128)}, f32[]{:T(128)}) all-reduce(f32[]{:T(128)} %get-tuple-element.3, f32[]{:T(128)} %get-tuple-element.2), channel_id=1, replica_groups=mesh['row'=32,'col'=8] {'row','col'}, use_global_device_ids=true, to_apply=%region_1.0 | all-reduce | flops 2 | bytes 16 | tf_op jit(solution)/shard_map/psum | solution.py:59
  295.1 1.0 multiply_reduce_fusion
  296.0 2.1 multiply_reduce_fusion.1
  298.1 73.5 %all-reduce = (f32[]{:T(128)}, f32[]{:T(128)}) all-reduce(f32[]{:T(128)} %get-tuple-element.9, f32[]{:T(128)} %multiply_reduce_fusion), channel_id=1, replica_groups=mesh['row'=32,'col'=8] {'row','col'}, use_global_device_ids=true, to_apply=%region_5.0 | all-reduce | flops 2 | bytes 16 | tf_op jit(solution)/shard_map/psum | solution.py:67
  373.0 0.6 pad_maximum_fusion
  373.6 1.0 broadcast_multiply_fusion
  (1 shorter events, 0.0 us)
Async XLA Ops:
  7.2 182.1 %copy-start = (f32[16,16]{1,0:T(8,128)S(1)}, f32[16,16]{1,0:T(8,128)}, u32[]{:S(2)}) copy-start(f32[16,16]{1,0:T(8,128)} %param.11) | copy-start | bytes 3076
  7.2 106.7 %all-gather.2.cloned.1.call-start = ((), (), s32[]{:S(2)}) async-start(), calls=%async_computation.3 | async-start | bytes 17301504 | tf_op jit(solution)/shard_map/all_gather | solution.py:55
  124.4 33.6 %copy-start.2 = (f32[256,1024]{1,0:T(8,128)}, f32[256,1024]{1,0:T(8,128)S(1)}, u32[]{:S(2)}) copy-start(f32[256,1024]{1,0:T(8,128)S(1)} %fusion) | copy-start | bytes 3145732
  158.0 30.9 %copy-start.3 = (s32[16,8192]{1,0:T(8,128)S(1)}, s32[16,8192]{1,0:T(8,128)}, u32[]{:S(2)}) copy-start(s32[16,8192]{1,0:T(8,128)} %param.9) | copy-start | bytes 1572868
  178.2 10.8 %copy-start.4 = (f32[16]{0:T(128)S(1)}, f32[16]{0:T(128)}, u32[]{:S(2)}) copy-start(f32[16]{0:T(128)} %param.10) | copy-start | bytes 196
  179.8 37.0 %copy-start.1 = (bf16[256,1024]{1,0:T(8,128)(2,1)S(1)}, bf16[256,1024]{1,0:T(8,128)(2,1)}, u32[]{:S(2)}) copy-start(bf16[256,1024]{1,0:T(8,128)(2,1)} %param.7) | copy-start | bytes 1572868
  179.8 35.5 %all-to-all-start.2 = ((f32[32,32,256]{2,1,0:T(8,128)}), f32[32,32,256]{2,1,0:T(8,128)S(1)}, u32[]{:S(2)}, u32[]{:S(2)}) async-start(f32[32,32,256]{2,1,0:T(8,128)} %bitcast.2), calls=%async_computation.2 | async-start | bytes 2097152 | tf_op jit(solution)/shard_map/all_to_all | solution.py:27
Sparse Core Ops, SparseCore 0:
  9.9 103.9 all-gather.1
where the time goes:
time: 382 us; the launch traced here: 381 us
  blocking collectives  202 us (53%)
  waiting for transfers between devices  104 us (27%)
  local copies, waits for them, and re-layouts  31.4 us (8%)
  between operations  16.9 us (4%)
  matrix products  13.1 us (3%)
  starting transfers between devices  9.11 us (2%)
  other arithmetic  5.93 us (2%)
    all_gather x1, waiting for transfers between devices, body(): lax.all_gather(coeff, 'row', axis=0, tiled=True)  77 us
    psum x1, blocking collectives, body(): lax.psum((jnp.sum(coeff_float * sigma), jnp.sum(coeff_float * coeff_float...  74.3 us
    psum x1, blocking collectives, body(): lax.psum((jnp.sum(residual * residual), jnp.sum(update * update)), ('row'...  73.5 us
    all_to_all x1, blocking collectives, turn_tiles(): lax.all_to_all(sectioned, 'row', split_axis=0, concat_axis=0, tiled=True)  33.6 us
    mul x2, local copies, waits for them, and re-layouts, body(): ham.reshape(mask_rows, block_size, mask_cols, block_size) * weights  28.3 us
    all_to_all x1, waiting for transfers between devices, turn_tiles(): lax.all_to_all(sectioned, 'row', split_axis=0, concat_axis=0, tiled=True)  25.9 us
    all_to_all x1, blocking collectives, turn_tiles(): lax.all_to_all(lax.all_to_all(sectioned, 'row', split_axis=0, concat_axis...  20.1 us
    dot_general x1, matrix products, body(): jnp.dot(masked, lax.all_gather(coeff, 'row', axis=0, tiled=True), preferr...  10.5 us
  transfers between devices with their start and end apart: 2, of which 2 were waited for; matrix products, arithmetic and copies ran while one was open for 8% of the time, Pallas kernels for 0%

commit v1 on v0

--- a/solution.py
+++ b/solution.py
@@ -52,7 +52,11 @@
     )
     diagonal = energy_alpha[:, None] + energy_beta[None, :] + coupling
     product = jnp.dot(
-        masked, lax.all_gather(coeff, "row", axis=0, tiled=True), preferred_element_type=jnp.float32
+        masked,
+        jnp.concatenate(
+            lax.all_to_all(jnp.stack([coeff] * lax.axis_size("row")), "row", 0, 0), axis=0
+        ),
+        preferred_element_type=jnp.float32,
     )
     coeff_float = coeff.astype(jnp.float32)
     sigma = product + turn_tiles(product)

time: 382 us -> 652 us (1.71)
  waiting for transfers between devices: 104 us -> 359 us
  between operations: 16.9 us -> 3.52 us
  starting transfers between devices: 9.11 us -> 20.3 us
  blocking collectives: 202 us -> 212 us
  local copies, waits for them, and re-layouts: 31.4 us -> 38 us
    all_to_all x0 -> x1, waiting for transfers between devices: none -> 333 us  [body(): lax.all_to_all(jnp.stack([coeff] * lax.axis_size('row')), 'row', 0, 0)]
    all_gather x1 -> x0, waiting for transfers between devices: 77 us -> none  [body(): lax.all_gather(coeff, 'row', axis=0, tiled=True)]
    all_to_all x0 -> x1, starting transfers between devices: none -> 11.2 us  [body(): lax.all_to_all(jnp.stack([coeff] * lax.axis_size('row')), 'row', 0, 0)]
    all_to_all x1, blocking collectives: 33.6 us -> 43.9 us  [turn_tiles(): lax.all_to_all(sectioned, 'row', split_axis=0, concat_axis=0, tiled=True)]
    another operation x0 -> x1, local copies, waits for them, and re-layouts: none -> 6.81 us  [body(): jnp.stack([coeff] * lax.axis_size('row'))]
  transfers between devices with their start and end apart: 2 -> 2, of which waited for: 2 -> 2; matrix products, arithmetic and copies ran while one was open for 8% -> 4% of each run, Pallas kernels for 0% -> 0%
where the time goes in v1:
time: 652 us; the launch traced here: 651 us
  waiting for transfers between devices  359 us (55%)
  blocking collectives  212 us (33%)
  local copies, waits for them, and re-layouts  38 us (6%)
  starting transfers between devices  20.3 us (3%)
  matrix products  13.1 us (2%)
    all_to_all x1, waiting for transfers between devices, body(): lax.all_to_all(jnp.stack([coeff] * lax.axis_size('row')), 'row', 0, 0)  333 us
    psum x1, blocking collectives, body(): lax.psum((jnp.sum(coeff_float * sigma), jnp.sum(coeff_float * coeff_float...  74.3 us
    psum x1, blocking collectives, body(): lax.psum((jnp.sum(residual * residual), jnp.sum(update * update)), ('row'...  73.5 us
    all_to_all x1, blocking collectives, turn_tiles(): lax.all_to_all(sectioned, 'row', split_axis=0, concat_axis=0, tiled=True)  43.9 us
    mul x2, local copies, waits for them, and re-layouts, body(): ham.reshape(mask_rows, block_size, mask_cols, block_size) * weights  28.1 us
    all_to_all x1, waiting for transfers between devices, turn_tiles(): lax.all_to_all(sectioned, 'row', split_axis=0, concat_axis=0, tiled=True)  25.9 us
    all_to_all x1, blocking collectives, turn_tiles(): lax.all_to_all(lax.all_to_all(sectioned, 'row', split_axis=0, concat_axis...  20.4 us
  transfers between devices with their start and end apart: 2, of which 2 were waited for; matrix products, arithmetic and copies ran while one was open for 4% of the time, Pallas kernels for 0%

profile of v1, /device:TPU:1, one launch (start us, length us, event | category | flops | bytes accessed | tf_op | source)
XLA Modules:
  0.0 651.0 jit_solution(2966094266446759296)
XLA Ops:
  0.6 0.0 copy-start
  0.6 6.8 %stack.8 = bf16[32,256,1024]{2,1,0:T(8,128)(2,1)} broadcast(bf16[256,1024]{1,0:T(8,128)(2,1)} %param.7), dimensions={1,2} | broadcast | bytes 17301504 | tf_op jit(solution)/shard_map/stack | solution.py:57
  7.5 0.0 copy-start.4
  7.5 11.2 %all-to-all-start = ((bf16[32,256,1024]{2,1,0:T(8,128)(2,1)}), bf16[32,256,1024]{2,1,0:T(8,128)(2,1)}, u32[]{:S(2)}, u32[]{:S(2)}) async-start(bf16[32,256,1024]{2,1,0:T(8,128)(2,1)} %stack.8), calls=%async_computation | async-start | bytes 33554432 | tf_op jit(solution)/shard_map/all_to_all | solution.py:57
  18.7 0.0 copy-done.4
  18.7 6.4 mul.41
  25.1 21.7 %mul.42 = bf16[256,8192]{1,0:T(8,128)(2,1)} reshape(bf16[8,32,256,32]{3,2,1,0:T(8,128)(2,1)} %mul.41) | data formatting | bytes 8388608 | tf_op jit(solution)/shard_map/mul | solution.py:40
  46.8 333.0 %all-to-all-done = bf16[32,256,1024]{2,1,0:T(8,128)(2,1)} async-done(((bf16[32,256,1024]{2,1,0:T(8,128)(2,1)}), bf16[32,256,1024]{2,1,0:T(8,128)(2,1)}, u32[]{:S(2)}, u32[]{:S(2)}) %all-to-all-start) | async-done | bytes 16777248 | tf_op jit(solution)/shard_map/all_to_all | solution.py:57
  379.8 10.5 %fusion = f32[256,1024]{1,0:T(8,128)S(1)} fusion(bf16[8192,1024]{1,0:T(8,128)(2,1)} %bitcast, bf16[256,8192]{1,0:T(8,128)(2,1)} %param.6, bf16[256,8192]{1,0:T(8,128)(2,1)} %mul.42), kind=kOutput, calls=%fused_computation | convolution fusion | flops 4297064448 | bytes 26214400 | tf_op jit(solution)/shard_map/dot_general | solution.py:54
  390.3 0.0 copy-start.2
  390.3 43.9 %all_to_all.20 = f32[32,8,1024]{2,1,0:T(8,128)S(1)} all-to-all(f32[32,8,1024]{2,1,0:T(8,128)S(1)} %bitcast.26), channel_id=1, replica_groups=mesh['row'=32,'col'=8] {'row'}, dimensions={0} | all-to-all | bytes 2097152 | tf_op jit(solution)/shard_map/all_to_all | solution.py:17
  434.2 0.0 copy-done.2
  434.2 0.0 copy-start.3
  434.2 20.4 %all_to_all.21 = f32[32,8,1024]{2,1,0:T(8,128)S(1)} all-to-all(f32[32,8,1024]{2,1,0:T(8,128)S(1)} %all_to_all.20), channel_id=1, replica_groups=mesh['row'=32,'col'=8] {'col'}, dimensions={0} | all-to-all | bytes 2097152 | tf_op jit(solution)/shard_map/all_to_all | solution.py:16
  454.5 0.0 copy-start.5
  454.5 0.5 reshape.32
  455.0 1.2 copy.10
  456.2 0.0 copy-start.1
  456.2 9.1 %all-to-all-start.3 = ((f32[32,32,256]{2,1,0:T(8,128)}), f32[32,32,256]{2,1,0:T(8,128)S(1)}, u32[]{:S(2)}, u32[]{:S(2)}) async-start(f32[32,32,256]{2,1,0:T(8,128)} %bitcast.3), calls=%async_computation.3 | async-start | bytes 2097152 | tf_op jit(solution)/shard_map/all_to_all | solution.py:27
  465.3 0.0 copy-done.3
  465.4 0.0 copy-done.5
  465.4 0.1 fusion.14
  465.5 0.2 fusion.10
  465.7 0.0 copy-done
  465.7 0.2 fusion.12
  465.9 25.9 %all-to-all-done.3 = f32[32,32,256]{2,1,0:T(8,128)S(1)} async-done(((f32[32,32,256]{2,1,0:T(8,128)}), f32[32,32,256]{2,1,0:T(8,128)S(1)}, u32[]{:S(2)}, u32[]{:S(2)}) %all-to-all-start.3) | async-done | bytes 1048608 | tf_op jit(solution)/shard_map/all_to_all | solution.py:27
  491.8 0.1 copy.11
  491.9 1.3 copy.12
  493.2 0.0 copy-done.1
  493.2 2.6 fusion.7
  495.8 74.3 %all-reduce.1 = (f32[]{:T(128)}, f32[]{:T(128)}) all-reduce(f32[]{:T(128)} %get-tuple-element.3, f32[]{:T(128)} %get-tuple-element.2), channel_id=1, replica_groups=mesh['row'=32,'col'=8] {'row','col'}, use_global_device_ids=true, to_apply=%region_1.0 | all-reduce | flops 2 | bytes 16 | tf_op jit(solution)/shard_map/psum | solution.py:63
  571.4 1.0 multiply_reduce_fusion
  572.4 2.1 multiply_reduce_fusion.1
  574.5 73.5 %all-reduce = (f32[]{:T(128)}, f32[]{:T(128)}) all-reduce(f32[]{:T(128)} %get-tuple-element.9, f32[]{:T(128)} %multiply_reduce_fusion), channel_id=1, replica_groups=mesh['row'=32,'col'=8] {'row','col'}, use_global_device_ids=true, to_apply=%region_5.0 | all-reduce | flops 2 | bytes 16 | tf_op jit(solution)/shard_map/psum | solution.py:71
  649.4 0.6 pad_maximum_fusion
  649.9 1.0 broadcast_multiply_fusion
  (2 shorter events, 0.0 us)
Async XLA Ops:
  0.6 465.1 %copy-start = (f32[16,16]{1,0:T(8,128)S(1)}, f32[16,16]{1,0:T(8,128)}, u32[]{:S(2)}) copy-start(f32[16,16]{1,0:T(8,128)} %param.11) | copy-start | bytes 3076
  7.5 11.3 %copy-start.4 = (s32[8,256]{1,0:T(8,128)S(1)}, s32[8,256]{1,0:T(8,128)}, u32[]{:S(2)}) copy-start(s32[8,256]{1,0:T(8,128)} %param.8) | copy-start | bytes 24580
  7.5 372.3 %all-to-all-start = ((bf16[32,256,1024]{2,1,0:T(8,128)(2,1)}), bf16[32,256,1024]{2,1,0:T(8,128)(2,1)}, u32[]{:S(2)}, u32[]{:S(2)}) async-start(bf16[32,256,1024]{2,1,0:T(8,128)(2,1)} %stack.8), calls=%async_computation | async-start | bytes 33554432 | tf_op jit(solution)/shard_map/all_to_all | solution.py:57
  390.3 43.9 %copy-start.2 = (f32[256,1024]{1,0:T(8,128)}, f32[256,1024]{1,0:T(8,128)S(1)}, u32[]{:S(2)}) copy-start(f32[256,1024]{1,0:T(8,128)S(1)} %fusion) | copy-start | bytes 3145732
  434.2 31.1 %copy-start.3 = (s32[16,8192]{1,0:T(8,128)S(1)}, s32[16,8192]{1,0:T(8,128)}, u32[]{:S(2)}) copy-start(s32[16,8192]{1,0:T(8,128)} %param.9) | copy-start | bytes 1572868
  454.5 10.8 %copy-start.5 = (f32[16]{0:T(128)S(1)}, f32[16]{0:T(128)}, u32[]{:S(2)}) copy-start(f32[16]{0:T(128)} %param.10) | copy-start | bytes 196
  456.2 37.0 %copy-start.1 = (bf16[256,1024]{1,0:T(8,128)(2,1)S(1)}, bf16[256,1024]{1,0:T(8,128)(2,1)}, u32[]{:S(2)}) copy-start(bf16[256,1024]{1,0:T(8,128)(2,1)} %param.7) | copy-start | bytes 1572868
  456.2 35.5 %all-to-all-start.3 = ((f32[32,32,256]{2,1,0:T(8,128)}), f32[32,32,256]{2,1,0:T(8,128)S(1)}, u32[]{:S(2)}, u32[]{:S(2)}) async-start(f32[32,32,256]{2,1,0:T(8,128)} %bitcast.3), calls=%async_computation.3 | async-start | bytes 2097152 | tf_op jit(solution)/shard_map/all_to_all | solution.py:27
